TPU v7x, 256 devices: a whole 4x4x8 slice. The times are simulated.
256 devices in a mesh: bx: 16 (over y, x_hi, core), by: 16 (over z, x_lo).
Axes of the slice: x: 4 (x_hi: 2, x_lo: 2; x = x_hi * 2 + x_lo), y: 4, z: 8, core: 2. Of those that a mesh axis runs over, the one named last changes fastest.
Arguments:
- points: bfloat16 [16, 16384, 512], P('by', 'bx'), may hold values from -6 to 6
- voxel_index: int32 [16, 16384], P('by', 'bx'), may hold values from 0 to 2047, as said below
- counts: int32 [16, 16], P('by', 'bx'), may hold values from 576 to 1024, as said below
- cpe_depth: bfloat16 [27, 512], replicated, may hold values from -2.5 to 2.5
- cpe_weight: bfloat16 [512, 512], replicated, may hold values from -0.25 to 0.25
- cpe_gain: bfloat16 [512], replicated, may hold values from 0.099609375 to 1.8984375
- norm1_gain: bfloat16 [512], replicated, may hold values from 0.099609375 to 1.8984375
- qkv_weight: bfloat16 [512, 1536], replicated
- proj_weight: bfloat16 [512, 512], replicated, may hold values from -0.25 to 0.25
- norm2_gain: bfloat16 [512], replicated, may hold values from 0.099609375 to 1.8984375
- mlp_in: bfloat16 [512, 2048], replicated, may hold values from -0.25 to 0.25
- mlp_out: bfloat16 [2048, 512], replicated, may hold values from -0.125 to 0.125
Outputs:
- block_out: bfloat16 [16, 16384, 512], P('by', 'bx')
Inputs may be any that keep to these rules, and one draw needn't show every extreme that they name: `voxel_index`: within one brick the 1024 slots name different voxels. `counts`: some brick of every chain is full.
All inputs are finite; a program needn't handle non-finite values.
Results may differ from a plain program's by a relative error of at most 0.012.
The roundings to bfloat16 on the way count: a program that leaves them out, or rounds other values in their place, can miss the bound.
Values may be sent and summed in bfloat16 or wider, within the bound.
A program may use at most 128 MiB of HBM per device.

v0:
```python
import jax
import jax.numpy as jnp
from jax import lax
from jax.experimental import pallas as pl
from jax.experimental.pallas import tpu as pltpu
from jax.sharding import PartitionSpec as P

MESH = pl.DeviceIdType.MESH
BF = jnp.bfloat16
F32 = jnp.float32
C = 512
HEADS = 32
ROWS = 1024
HALF = 512
VX = 8
VY = 16
VZ = 16
VOX = 2048
PLANE = VY * VZ
NEG = -1e30
CQ = 256
UNROLL = 4


def dot(a, b):
    return jnp.dot(a, b, preferred_element_type=F32)


def dot_nt(a, b):
    return lax.dot_general(a, b, (((1,), (1,)), ((), ())), preferred_element_type=F32)


def dot_tn(a, b):
    return lax.dot_general(a, b, (((0,), (0,)), ((), ())), preferred_element_type=F32)


def layer_norm(values):
    center = values - jnp.mean(values, axis=-1, keepdims=True)
    spread = jnp.mean(center * center, axis=-1, keepdims=True)
    return center * lax.rsqrt(spread + 1e-05)


def front_kernel(
    points,
    voxels,
    counts,
    depth,
    cpe_w_hbm,
    cpe_gain,
    gain1,
    qkv_hbm,
    proj_hbm,
    second,
    feats,
    cpe_w,
    qkv_w,
    proj_w,
    wt,
    grid,
    taps,
    conv,
    first,
    normed,
    far,
    qt,
    keys,
    vt,
    far_keys,
    far_vt,
    bias,
    ones_row,
    scores,
    tops,
    part_o,
    part_ml,
    att,
    count_out,
    count_in,
    load_sem,
    send_sem,
    recv_sem,
):
    bx, by = lax.axis_index("bx"), lax.axis_index("by")
    n_bx, n_by = lax.axis_size("bx"), lax.axis_size("by")
    low_x, high_x = lax.rem(bx + n_bx - 1, n_bx), lax.rem(bx + 1, n_bx)
    low_y, high_y = lax.rem(by + n_by - 1, n_by), lax.rem(by + 1, n_by)

    def at(x, y):
        return {"bx": x, "by": y}

    around = [
        (low_x, by),
        (high_x, by),
        (bx, low_y),
        (bx, high_y),
        (low_x, low_y),
        (low_x, high_y),
        (high_x, low_y),
        (high_x, high_y),
    ]
    barrier = pltpu.get_barrier_semaphore()
    for x, y in around:
        pl.semaphore_signal(barrier, inc=1, device_id=at(x, y), device_id_type=MESH)

    loads = [
        pltpu.make_async_copy(source, held, load_sem.at[i])
        for i, (source, held) in enumerate(
            (
                (points.at[0], feats),
                (cpe_w_hbm, cpe_w),
                (qkv_hbm, qkv_w),
                (proj_hbm, proj_w),
            )
        )
    ]
    for load in loads:
        load.start()

    def remote(i, source, target, where):
        return pltpu.make_async_remote_copy(
            src_ref=source,
            dst_ref=target,
            send_sem=send_sem.at[i],
            recv_sem=recv_sem.at[i],
            device_id=at(*where),
            device_id_type=MESH,
        )

    inner_y = pl.ds(1, VY)
    inner_x = pl.ds(1, VX)
    halo_x = [
        remote(0, grid.at[1, inner_y], grid.at[VX + 1, inner_y], (low_x, by)),
        remote(1, grid.at[VX, inner_y], grid.at[0, inner_y], (high_x, by)),
        remote(2, grid.at[1, 1], grid.at[VX + 1, VY + 1], (low_x, low_y)),
        remote(3, grid.at[1, VY], grid.at[VX + 1, 0], (low_x, high_y)),
        remote(4, grid.at[VX, 1], grid.at[0, VY + 1], (high_x, low_y)),
        remote(5, grid.at[VX, VY], grid.at[0, 0], (high_x, high_y)),
        remote(6, count_out, count_in, (high_x, by)),
    ]
    halo_y = [
        remote(7, grid.at[inner_x, 1], grid.at[inner_x, VY + 1], (bx, low_y)),
        remote(8, grid.at[inner_x, VY], grid.at[inner_x, 0], (bx, high_y)),
    ]
    low_half, high_half = pl.ds(0, HALF), pl.ds(HALF, HALF)
    to_low = remote(9, normed.at[low_half], far.at[high_half], (low_x, by))
    to_high = remote(10, normed.at[high_half], far.at[low_half], (high_x, by))

    count = counts[...].astype(F32)
    count_out[...] = jnp.broadcast_to(count, (8, 128))
    slot = lax.broadcasted_iota(jnp.int32, (1, ROWS), 1)
    where_to = jnp.where(slot.astype(F32) < count, voxels[...], VOX)

    loads[0].wait()

    def scatter(plane):
        row = lax.broadcasted_iota(jnp.int32, (PLANE, ROWS), 0) + plane * PLANE
        hot = jnp.where(row == where_to, 1.0, 0.0).astype(BF)
        grid[plane + 1, 1 : VY + 1] = dot(hot, feats[...]).astype(BF).reshape(VY, VZ, C)

    scatter(0)
    scatter(VX - 1)
    pl.semaphore_wait(barrier, 8)
    for copy in halo_x:
        copy.start()

    def scatter_step(plane, carry):
        scatter(plane)
        return carry

    lax.fori_loop(1, VX - 1, scatter_step, 0)
    for copy in halo_y:
        copy.start()

    taps[...] = depth[...].astype(F32)

    def conv_rows(x, lanes, y_first, y_count):
        weight = [taps[pl.ds(i, 1), lanes] for i in range(27)]
        z = lax.broadcasted_iota(jnp.int32, (VZ, 128), 0)
        parts = [[None] * 3 for _ in range(y_count)]
        for off_x in range(3):
            for row in range(y_count + 2):
                block = grid[x + off_x, y_first + row, :, lanes].astype(F32)
                for i in range(y_count):
                    off_y = row - i
                    if 0 <= off_y <= 2:
                        for off_z in range(3):
                            term = block * weight[9 * off_x + 3 * off_y + off_z]
                            held = parts[i][off_z]
                            parts[i][off_z] = term if held is None else held + term
        for i in range(y_count):
            before, same, after = parts[i]
            before = jnp.where(z == 0, 0.0, pltpu.roll(before, 1, 0))
            after = jnp.where(z == VZ - 1, 0.0, pltpu.roll(after, VZ - 1, 0))
            start = pl.multiple_of(x * PLANE + (y_first + i) * VZ, VZ)
            conv[pl.ds(start, VZ), lanes] = (before + same + after).astype(BF)

    def inner_step(i, carry):
        lanes = pl.ds(pl.multiple_of(lax.rem(i, 4) * 128, 128), 128)
        for y in range(1, VY - 1, 2):
            conv_rows(lax.div(i, 4) + 1, lanes, y, 2)
        return carry

    lax.fori_loop(0, 4 * (VX - 2), inner_step, 0)

    loads[1].wait()
    loads[2].wait()
    loads[3].wait()
    wt[0:C] = qkv_w[:, 0:C].T
    wt[C : 2 * C] = qkv_w[:, 2 * C : 3 * C].T

    for copy in halo_x + halo_y:
        copy.wait()
    zero_x = jnp.zeros((VY + 2, VZ, C), BF)
    zero_y = jnp.zeros((VX + 2, VZ, C), BF)

    @pl.when(bx == 0)
    def _():
        grid[0] = zero_x

    @pl.when(bx == n_bx - 1)
    def _():
        grid[VX + 1] = zero_x

    @pl.when(by == 0)
    def _():
        grid[:, 0] = zero_y

    @pl.when(by == n_by - 1)
    def _():
        grid[:, VY + 1] = zero_y

    def outer_step(i, carry):
        lanes = pl.ds(pl.multiple_of(lax.rem(i, 4) * 128, 128), 128)
        for y in range(0, VY, 2):
            conv_rows(lax.div(i, 4) * (VX - 1), lanes, y, 2)
        return carry

    lax.fori_loop(0, 8, outer_step, 0)

    def side_step(i, carry):
        lanes = pl.ds(pl.multiple_of(lax.rem(i, 4) * 128, 128), 128)
        for y in (0, VY - 1):
            conv_rows(lax.div(i, 4) + 1, lanes, y, 1)
        return carry

    lax.fori_loop(0, 4 * (VX - 2), side_step, 0)

    def gather(half):
        total = None
        for part in range(4):
            lane = lax.broadcasted_iota(jnp.int32, (HALF, HALF), 1) + part * HALF
            column = jnp.concatenate(
                [
                    jnp.broadcast_to(
                        voxels[:, half * HALF + i * 128 : half * HALF + (i + 1) * 128].astype(F32),
                        (128, 128),
                    ).T
                    for i in range(4)
                ],
                axis=0,
            ).astype(jnp.int32)
            hot = jnp.where(jnp.concatenate([column] * 4, axis=1) == lane, 1.0, 0.0).astype(BF)
            term = dot(hot, conv[part * HALF : (part + 1) * HALF])
            total = term if total is None else total + term
        rows = slice(half * HALF, (half + 1) * HALF)
        branch = layer_norm(dot(total.astype(BF), cpe_w[...])) * cpe_gain[...].astype(F32)
        here = (feats[rows].astype(F32) + branch).astype(BF)
        first[rows] = here
        normed[rows] = (layer_norm(here.astype(F32)) * gain1[...].astype(F32)).astype(BF)

    gather(0)
    to_low.start()
    gather(1)
    to_high.start()

    qt[...] = (dot_nt(wt[0:C], normed[...]).astype(BF).astype(F32) * 0.25).astype(BF)
    keys[...] = dot(normed[...], qkv_w[:, C : 2 * C]).astype(BF)
    vt[...] = dot_nt(wt[C : 2 * C], normed[...]).astype(BF)

    row_id = (lax.broadcasted_iota(jnp.int32, (HALF, 128), 0) + HALF).astype(F32)
    lane_id = lax.broadcasted_iota(jnp.int32, (HALF, 128), 1)
    bias[0] = jnp.where((lane_id == 0) & (row_id >= count), NEG, 0.0).astype(BF)
    bias[1] = jnp.where((lane_id == 0) & (row_id >= count_in[0:1, :]), NEG, 0.0).astype(BF)
    ones_row[...] = jnp.where(
        lax.broadcasted_iota(jnp.int32, (128, CQ), 0) == 0, 1.0, 0.0
    ).astype(BF)

    lane_head = lax.broadcasted_iota(jnp.int32, (1, 128), 1) // 16
    ones16 = jnp.ones((16, HALF), BF)

    def attention(k_ref, v_ref, biased, which, finish):
        def step(h, before, now):
            other = 1 - now
            lanes = pl.ds(pl.multiple_of(lax.div(h, 8) * 128, 128), 128)
            mine = lane_head == lax.rem(h, 8)
            if before is not None:
                head_rows = pl.ds(pl.multiple_of(before * 16, 16), 16)
            for b in range(2):
                rows = slice(b * HALF, (b + 1) * HALF)
                k_h = k_ref[rows, lanes]
                k_h = jnp.where(mine, k_h, jnp.zeros_like(k_h))
                if b == biased:
                    k_h = jnp.concatenate([k_h, bias[which]], axis=1)
                if before is not None:
                    w = jnp.concatenate([v_ref[head_rows, rows], ones16], axis=0)
                for part in range(HALF // CQ):
                    cols = slice(b * HALF + part * CQ, b * HALF + (part + 1) * CQ)
                    q_g = qt[lanes, cols]
                    if b == biased:
                        q_g = jnp.concatenate([q_g, ones_row[...]], axis=0)
                    s = dot(k_h, q_g)
                    scores[now, :, cols] = s
                    tops[now, 0:1, cols] = jnp.max(s, axis=0, keepdims=True)
                    if before is not None:
                        top = tops[other, 0:1, cols]
                        p = jnp.exp(scores[other, :, cols] - top).astype(BF)
                        finish(before, head_rows, cols, top, dot(w, p))

        step(0, None, 0)

        def body(i, carry):
            for u in range(UNROLL):
                before = i * UNROLL + u
                step(jnp.minimum(before + 1, HEADS - 1), before, (u + 1) % 2)
            return carry

        lax.fori_loop(0, HEADS // UNROLL, body, 0)

    def keep(h, head_rows, cols, top, acc):
        part_o[head_rows, cols] = acc[0:16]
        part_ml[h, 0:1, cols] = top
        part_ml[h, 1:2, cols] = acc[16:17]

    attention(keys, vt, 1, 0, keep)

    to_low.wait()
    to_high.wait()
    far_keys[...] = dot(far[...], qkv_w[:, C : 2 * C]).astype(BF)
    far_vt[...] = dot_nt(wt[C : 2 * C], far[...]).astype(BF)

    def merge(h, head_rows, cols, top, acc):
        near_top = part_ml[h, 0:1, cols]
        both = jnp.maximum(near_top, top)
        near, here = jnp.exp(near_top - both), jnp.exp(top - both)
        total = part_ml[h, 1:2, cols] * near + acc[16:17] * here
        att[head_rows, cols] = ((part_o[head_rows, cols] * near + acc[0:16] * here) / total).astype(BF)

    attention(far_keys, far_vt, 0, 1, merge)

    second[...] = (first[...].astype(F32) + dot_tn(att[...], proj_w[...])).astype(BF)


def erf(x):
    size = jnp.abs(x)
    t = 1.0 / (1.0 + 0.3275911 * size)
    poly = t * (
        0.254829592
        + t * (-0.284496736 + t * (1.421413741 + t * (-1.453152027 + t * 1.061405429)))
    )
    value = 1.0 - poly * jnp.exp(-size * size)
    return jnp.where(x < 0, -value, value)


def gelu(x):
    return 0.5 * x * (1.0 + erf(x * 0.7071067811865476))


def back_kernel(second, counts, gain2, mlp_in, mlp_out, out):
    tile = 256
    count = counts[...].astype(F32)

    def step(i, carry):
        rows = pl.ds(pl.multiple_of(i * tile, tile), tile)
        here = second[rows, :].astype(F32)
        normed = (layer_norm(here) * gain2[...].astype(F32)).astype(BF)
        total = here
        for part in range(4):
            cols = slice(part * 512, (part + 1) * 512)
            hidden = gelu(dot(normed, mlp_in[:, cols])).astype(BF)
            total = total + dot(hidden, mlp_out[cols, :])
        row_id = (lax.broadcasted_iota(jnp.int32, (tile, C), 0) + i * tile).astype(F32)
        out[0, rows, :] = jnp.where(row_id < count, total, 0.0).astype(BF)
        return carry

    lax.fori_loop(0, ROWS // tile, step, 0)


def per_device(
    points,
    voxel_index,
    counts,
    cpe_depth,
    cpe_weight,
    cpe_gain,
    norm1_gain,
    qkv_weight,
    proj_weight,
    norm2_gain,
    mlp_in,
    mlp_out,
):
    vmem = pl.BlockSpec(memory_space=pltpu.VMEM)
    hbm = pl.BlockSpec(memory_space=pl.ANY)
    second = pl.pallas_call(
        front_kernel,
        out_shape=jax.ShapeDtypeStruct((ROWS, C), BF),
        in_specs=[hbm, vmem, vmem, vmem, hbm, vmem, vmem, hbm, hbm],
        out_specs=vmem,
        scratch_shapes=[
            pltpu.VMEM((ROWS, C), BF),
            pltpu.VMEM((C, C), BF),
            pltpu.VMEM((C, 3 * C), BF),
            pltpu.VMEM((C, C), BF),
            pltpu.VMEM((2 * C, C), BF),
            pltpu.VMEM((VX + 2, VY + 2, VZ, C), BF),
            pltpu.VMEM((27, C), F32),
            pltpu.VMEM((VOX, C), BF),
            pltpu.VMEM((ROWS, C), BF),
            pltpu.VMEM((ROWS, C), BF),
            pltpu.VMEM((ROWS, C), BF),
            pltpu.VMEM((C, ROWS), BF),
            pltpu.VMEM((ROWS, C), BF),
            pltpu.VMEM((C, ROWS), BF),
            pltpu.VMEM((ROWS, C), BF),
            pltpu.VMEM((C, ROWS), BF),
            pltpu.VMEM((2, HALF, 128), BF),
            pltpu.VMEM((128, CQ), BF),
            pltpu.VMEM((2, HALF, ROWS), F32),
            pltpu.VMEM((2, 8, ROWS), F32),
            pltpu.VMEM((C, ROWS), F32),
            pltpu.VMEM((HEADS, 8, ROWS), F32),
            pltpu.VMEM((C, ROWS), BF),
            pltpu.VMEM((8, 128), F32),
            pltpu.VMEM((8, 128), F32),
            pltpu.SemaphoreType.DMA((4,)),
            pltpu.SemaphoreType.DMA((11,)),
            pltpu.SemaphoreType.DMA((11,)),
        ],
        compiler_params=pltpu.CompilerParams(
            collective_id=0, has_side_effects=True, vmem_limit_bytes=48 * 2**20
        ),
        name="front",
    )(
        points,
        voxel_index,
        counts,
        cpe_depth,
        cpe_weight,
        cpe_gain.reshape(1, C),
        norm1_gain.reshape(1, C),
        qkv_weight,
        proj_weight,
    )
    return pl.pallas_call(
        back_kernel,
        out_shape=jax.ShapeDtypeStruct((1, ROWS, C), BF),
        in_specs=[vmem] * 5,
        out_specs=vmem,
        compiler_params=pltpu.CompilerParams(vmem_limit_bytes=48 * 2**20),
        name="back",
    )(second, counts, norm2_gain.reshape(1, C), mlp_in, mlp_out)


def solution(mesh):
    in_specs = (P("by", "bx", None), P("by", "bx"), P("by", "bx")) + (P(),) * 9
    return jax.shard_map(
        per_device,
        mesh=mesh,
        in_specs=in_specs,
        out_specs=P("by", "bx", None),
        check_vma=False,
    )
```

profile of v0, /device:TPU:1, one launch (start us, length us, event | category | flops | bytes accessed | tf_op | source)
XLA Modules:
  0.0 86.2 jit_solution(4202941297490519016)
XLA Ops:
  0.7 0.7 reshape.9.cpe_gain
  1.3 0.7 reshape.10.gain1
  2.0 0.7 reshape.11.gain2
  2.7 0.0 copy-start.2
  2.7 1.4 %copy-done.2 = bf16[512,1536]{1,0:T(8,128)(2,1)S(1)} copy-done((bf16[512,1536]{1,0:T(8,128)(2,1)S(1)}, bf16[512,1536]{1,0:T(8,128)(2,1)}, u32[]{:S(2)}) %copy-start.2) | copy-done | bytes 1572888
  4.1 0.0 copy-start.3
  4.1 1.2 %copy-done.3 = bf16[1,1024,512]{2,1,0:T(8,128)(2,1)S(1)} copy-done((bf16[1,1024,512]{2,1,0:T(8,128)(2,1)S(1)}, bf16[1,1024,512]{2,1,0:T(8,128)(2,1)}, u32[]{:S(2)}) %copy-start.3) | copy-done | bytes 1048600
  5.3 0.0 copy-start.4
  5.3 1.0 %copy-done.4 = bf16[512,512]{1,0:T(8,128)(2,1)S(1)} copy-done((bf16[512,512]{1,0:T(8,128)(2,1)S(1)}, bf16[512,512]{1,0:T(8,128)(2,1)}, u32[]{:S(2)}) %copy-start.4) | copy-done | bytes 524312
  6.4 0.0 copy-start.5
  6.4 1.0 %copy-done.5 = bf16[512,512]{1,0:T(8,128)(2,1)S(1)} copy-done((bf16[512,512]{1,0:T(8,128)(2,1)S(1)}, bf16[512,512]{1,0:T(8,128)(2,1)}, u32[]{:S(2)}) %copy-start.5) | copy-done | bytes 524312
  7.4 0.0 copy-start.6
  7.4 0.8 copy-done.6
  8.2 0.0 copy-start.7
  8.2 0.7 copy-done.7
  8.9 0.0 copy-start
  8.9 0.0 copy-start.1
  8.9 62.7 %front.1.second = bf16[1024,512]{1,0:T(8,128)(2,1)S(1)} custom-call(bf16[1,1024,512]{2,1,0:T(8,128)(2,1)S(1)} %copy-done.3, s32[1,1024]{1,0:T(1,128)S(1)} %copy-done.7, s32[1,1]{1,0:T(1,128)S(6)} %copy.13.counts, bf16[27,512]{1,0:T(8,128)(2,1)S(1)} %copy-done.6, bf16[512,512]{1,0:T(8,128)(2,1)S(1)} %copy-done.4, bf16[1,512]{1,0:T(2,128)(2,1)S(1)} %reshape.9.cpe_gain, ...), custom_call_target="tpu_custom_call" | custom-call | tf_op jit(solution)/shard_map/front/pallas_call | solution.py:404
  71.6 0.0 copy-done
  71.6 0.0 copy-done.1
  71.6 14.6 %back.1 = bf16[1,1024,512]{2,1,0:T(8,128)(2,1)} custom-call(bf16[1024,512]{1,0:T(8,128)(2,1)S(1)} %front.1.second, s32[1,1]{1,0:T(1,128)S(6)} %copy.13.counts, bf16[1,512]{1,0:T(2,128)(2,1)S(1)} %reshape.11.gain2, bf16[512,2048]{1,0:T(8,128)(2,1)S(1)} %copy-done, bf16[2048,512]{1,0:T(8,128)(2,1)S(1)} %copy-done.1), custom_call_target="tpu_custom_call" | custom-call | tf_op jit(solution)/shard_map/back/pallas_call | solution.py:454
Async XLA Ops:
  2.7 1.4 %copy-start.2 = (bf16[512,1536]{1,0:T(8,128)(2,1)S(1)}, bf16[512,1536]{1,0:T(8,128)(2,1)}, u32[]{:S(2)}) copy-start(bf16[512,1536]{1,0:T(8,128)(2,1)} %qkv_hbm.1) | copy-start | bytes 4718596
  4.1 1.2 %copy-start.3 = (bf16[1,1024,512]{2,1,0:T(8,128)(2,1)S(1)}, bf16[1,1024,512]{2,1,0:T(8,128)(2,1)}, u32[]{:S(2)}) copy-start(bf16[1,1024,512]{2,1,0:T(8,128)(2,1)} %points.1) | copy-start | bytes 3145732
  5.3 1.0 %copy-start.4 = (bf16[512,512]{1,0:T(8,128)(2,1)S(1)}, bf16[512,512]{1,0:T(8,128)(2,1)}, u32[]{:S(2)}) copy-start(bf16[512,512]{1,0:T(8,128)(2,1)} %cpe_w_hbm.1) | copy-start | bytes 1572868
  6.4 1.0 %copy-start.5 = (bf16[512,512]{1,0:T(8,128)(2,1)S(1)}, bf16[512,512]{1,0:T(8,128)(2,1)}, u32[]{:S(2)}) copy-start(bf16[512,512]{1,0:T(8,128)(2,1)} %proj_hbm.1) | copy-start | bytes 1572868
  7.4 0.8 copy-start.6
  8.2 0.7 copy-start.7
  8.9 62.7 %copy-start = (bf16[512,2048]{1,0:T(8,128)(2,1)S(1)}, bf16[512,2048]{1,0:T(8,128)(2,1)}, u32[]{:S(2)}) copy-start(bf16[512,2048]{1,0:T(8,128)(2,1)} %mlp_in.1) | copy-start | bytes 6291460
  8.9 62.8 %copy-start.1 = (bf16[2048,512]{1,0:T(8,128)(2,1)S(1)}, bf16[2048,512]{1,0:T(8,128)(2,1)}, u32[]{:S(2)}) copy-start(bf16[2048,512]{1,0:T(8,128)(2,1)} %mlp_out.1) | copy-start | bytes 6291460
where the time goes:
time: 87.5 us; the launch traced here: 86.2 us
  Pallas kernels  77.3 us (88%)
  local copies, waits for them, and re-layouts  8.21 us (9%)
    pallas_call x1, Pallas kernels, per_device(): pl.pallas_call(front_kernel, out_shape=jax.ShapeDtypeStruct((ROWS, C), BF...  62.7 us
    pallas_call x1, Pallas kernels, per_device(): pl.pallas_call(back_kernel, out_shape=jax.ShapeDtypeStruct((1, ROWS, C),...  14.6 us
    unnamed x16, local copies, waits for them, and re-layouts  6.16 us

commit v1 on v0

--- a/solution.py
+++ b/solution.py
@@ -41,17 +41,25 @@
 
 
 def front_kernel(
-    points,
+    points_hbm,
+    voxels_hbm,
+    counts_hbm,
+    depth_hbm,
+    cpe_w_hbm,
+    cpe_gain_hbm,
+    gain1_hbm,
+    qkv_hbm,
+    proj_hbm,
+    gain2_hbm,
+    second,
+    aside,
+    feats,
     voxels,
     counts,
     depth,
-    cpe_w_hbm,
     cpe_gain,
     gain1,
-    qkv_hbm,
-    proj_hbm,
-    second,
-    feats,
+    gain2,
     cpe_w,
     qkv_w,
     proj_w,
@@ -106,7 +114,13 @@
         pltpu.make_async_copy(source, held, load_sem.at[i])
         for i, (source, held) in enumerate(
             (
-                (points.at[0], feats),
+                (voxels_hbm, voxels),
+                (counts_hbm, counts),
+                (points_hbm.at[0], feats),
+                (depth_hbm, depth),
+                (cpe_gain_hbm, cpe_gain),
+                (gain1_hbm, gain1),
+                (gain2_hbm, gain2),
                 (cpe_w_hbm, cpe_w),
                 (qkv_hbm, qkv_w),
                 (proj_hbm, proj_w),
@@ -145,12 +159,14 @@
     to_low = remote(9, normed.at[low_half], far.at[high_half], (low_x, by))
     to_high = remote(10, normed.at[high_half], far.at[low_half], (high_x, by))
 
+    loads[0].wait()
+    loads[1].wait()
     count = counts[...].astype(F32)
     count_out[...] = jnp.broadcast_to(count, (8, 128))
     slot = lax.broadcasted_iota(jnp.int32, (1, ROWS), 1)
     where_to = jnp.where(slot.astype(F32) < count, voxels[...], VOX)
 
-    loads[0].wait()
+    loads[2].wait()
 
     def scatter(plane):
         row = lax.broadcasted_iota(jnp.int32, (PLANE, ROWS), 0) + plane * PLANE
@@ -171,6 +187,7 @@
     for copy in halo_y:
         copy.start()
 
+    loads[3].wait()
     taps[...] = depth[...].astype(F32)
 
     def conv_rows(x, lanes, y_first, y_count):
@@ -202,9 +219,8 @@
 
     lax.fori_loop(0, 4 * (VX - 2), inner_step, 0)
 
-    loads[1].wait()
-    loads[2].wait()
-    loads[3].wait()
+    for load in loads[4:]:
+        load.wait()
     wt[0:C] = qkv_w[:, 0:C].T
     wt[C : 2 * C] = qkv_w[:, 2 * C : 3 * C].T
 
@@ -263,10 +279,10 @@
             term = dot(hot, conv[part * HALF : (part + 1) * HALF])
             total = term if total is None else total + term
         rows = slice(half * HALF, (half + 1) * HALF)
-        branch = layer_norm(dot(total.astype(BF), cpe_w[...])) * cpe_gain[...].astype(F32)
+        branch = layer_norm(dot(total.astype(BF), cpe_w[...])) * cpe_gain[...].reshape(1, C).astype(F32)
         here = (feats[rows].astype(F32) + branch).astype(BF)
         first[rows] = here
-        normed[rows] = (layer_norm(here.astype(F32)) * gain1[...].astype(F32)).astype(BF)
+        normed[rows] = (layer_norm(here.astype(F32)) * gain1[...].reshape(1, C).astype(F32)).astype(BF)
 
     gather(0)
     to_low.start()
@@ -276,6 +292,9 @@
     qt[...] = (dot_nt(wt[0:C], normed[...]).astype(BF).astype(F32) * 0.25).astype(BF)
     keys[...] = dot(normed[...], qkv_w[:, C : 2 * C]).astype(BF)
     vt[...] = dot_nt(wt[C : 2 * C], normed[...]).astype(BF)
+
+    aside[0:1, :] = gain2[...].reshape(1, C).astype(F32)
+    aside[1:2, :] = jnp.broadcast_to(count, (1, C))
 
     row_id = (lax.broadcasted_iota(jnp.int32, (HALF, 128), 0) + HALF).astype(F32)
     lane_id = lax.broadcasted_iota(jnp.int32, (HALF, 128), 1)
@@ -350,39 +369,20 @@
     second[...] = (first[...].astype(F32) + dot_tn(att[...], proj_w[...])).astype(BF)
 
 
-def erf(x):
-    size = jnp.abs(x)
-    t = 1.0 / (1.0 + 0.3275911 * size)
-    poly = t * (
-        0.254829592
-        + t * (-0.284496736 + t * (1.421413741 + t * (-1.453152027 + t * 1.061405429)))
-    )
-    value = 1.0 - poly * jnp.exp(-size * size)
-    return jnp.where(x < 0, -value, value)
-
-
 def gelu(x):
-    return 0.5 * x * (1.0 + erf(x * 0.7071067811865476))
-
-
-def back_kernel(second, counts, gain2, mlp_in, mlp_out, out):
-    tile = 256
-    count = counts[...].astype(F32)
-
-    def step(i, carry):
-        rows = pl.ds(pl.multiple_of(i * tile, tile), tile)
-        here = second[rows, :].astype(F32)
-        normed = (layer_norm(here) * gain2[...].astype(F32)).astype(BF)
-        total = here
-        for part in range(4):
-            cols = slice(part * 512, (part + 1) * 512)
-            hidden = gelu(dot(normed, mlp_in[:, cols])).astype(BF)
-            total = total + dot(hidden, mlp_out[cols, :])
-        row_id = (lax.broadcasted_iota(jnp.int32, (tile, C), 0) + i * tile).astype(F32)
-        out[0, rows, :] = jnp.where(row_id < count, total, 0.0).astype(BF)
-        return carry
-
-    lax.fori_loop(0, ROWS // tile, step, 0)
+    half = 0.5 * x
+    return half + half * lax.erf(x * 0.7071067811865476)
+
+
+def back_kernel(second, aside, mlp_in, mlp_out, out):
+    total = second[...].astype(F32)
+    normed = (layer_norm(total) * aside[0:1, :]).astype(BF)
+    for part in range(4):
+        cols = slice(part * 512, (part + 1) * 512)
+        hidden = gelu(dot(normed, mlp_in[:, cols])).astype(BF)
+        total = total + dot(hidden, mlp_out[cols, :])
+    row_id = lax.broadcasted_iota(jnp.int32, (ROWS, C), 0).astype(F32)
+    out[0] = jnp.where(row_id < aside[1:2, :], total, 0.0).astype(BF)
 
 
 def per_device(
@@ -401,13 +401,22 @@
 ):
     vmem = pl.BlockSpec(memory_space=pltpu.VMEM)
     hbm = pl.BlockSpec(memory_space=pl.ANY)
-    second = pl.pallas_call(
+    second, aside = pl.pallas_call(
         front_kernel,
-        out_shape=jax.ShapeDtypeStruct((ROWS, C), BF),
-        in_specs=[hbm, vmem, vmem, vmem, hbm, vmem, vmem, hbm, hbm],
-        out_specs=vmem,
+        out_shape=(
+            jax.ShapeDtypeStruct((ROWS, C), BF),
+            jax.ShapeDtypeStruct((8, C), F32),
+        ),
+        in_specs=[hbm] * 10,
+        out_specs=(vmem, vmem),
         scratch_shapes=[
             pltpu.VMEM((ROWS, C), BF),
+            pltpu.VMEM((1, ROWS), jnp.int32),
+            pltpu.VMEM((1, 1), jnp.int32),
+            pltpu.VMEM((27, C), BF),
+            pltpu.VMEM((C,), BF),
+            pltpu.VMEM((C,), BF),
+            pltpu.VMEM((C,), BF),
             pltpu.VMEM((C, C), BF),
             pltpu.VMEM((C, 3 * C), BF),
             pltpu.VMEM((C, C), BF),
@@ -432,7 +441,7 @@
             pltpu.VMEM((C, ROWS), BF),
             pltpu.VMEM((8, 128), F32),
             pltpu.VMEM((8, 128), F32),
-            pltpu.SemaphoreType.DMA((4,)),
+            pltpu.SemaphoreType.DMA((10,)),
             pltpu.SemaphoreType.DMA((11,)),
             pltpu.SemaphoreType.DMA((11,)),
         ],
@@ -446,19 +455,20 @@
         counts,
         cpe_depth,
         cpe_weight,
-        cpe_gain.reshape(1, C),
-        norm1_gain.reshape(1, C),
+        cpe_gain,
+        norm1_gain,
         qkv_weight,
         proj_weight,
+        norm2_gain,
     )
     return pl.pallas_call(
         back_kernel,
         out_shape=jax.ShapeDtypeStruct((1, ROWS, C), BF),
-        in_specs=[vmem] * 5,
+        in_specs=[vmem] * 4,
         out_specs=vmem,
         compiler_params=pltpu.CompilerParams(vmem_limit_bytes=48 * 2**20),
         name="back",
-    )(second, counts, norm2_gain.reshape(1, C), mlp_in, mlp_out)
+    )(second, aside, mlp_in, mlp_out)
 
 
 def solution(mesh):

time: 87.5 us -> 81.9 us (0.936)
  Pallas kernels: 77.3 us -> 70 us
  local copies, waits for them, and re-layouts: 8.21 us -> 9.78 us
    pallas_call x1, Pallas kernels: 14.6 us -> 6.07 us  [per_device(): pl.pallas_call(back_kernel, out_shape=jax.ShapeDtypeStruct((1, ROWS, C),...]
    unnamed x16 -> x22, local copies, waits for them, and re-layouts: 6.16 us -> 9.78 us
    reshape x3 -> x0, local copies, waits for them, and re-layouts: 2.05 us -> none  [the longest x1 0.68 us: per_device(): cpe_gain.reshape(1, C)]
    pallas_call x1, Pallas kernels: 62.7 us -> 63.9 us  [per_device(): pl.pallas_call(front_kernel, out_shape=(jax.ShapeDtypeStruct((ROWS, C), B...]
where the time goes in v1:
time: 81.9 us; the launch traced here: 80.6 us
  Pallas kernels  70 us (85%)
  local copies, waits for them, and re-layouts  9.78 us (12%)
  between operations  0.84 us (1%)
    pallas_call x1, Pallas kernels, per_device(): pl.pallas_call(front_kernel, out_shape=(jax.ShapeDtypeStruct((ROWS, C), B...  63.9 us
    unnamed x22, local copies, waits for them, and re-layouts  9.78 us
    pallas_call x1, Pallas kernels, per_device(): pl.pallas_call(back_kernel, out_shape=jax.ShapeDtypeStruct((1, ROWS, C),...  6.07 us

profile of v1, /device:TPU:1, one launch (start us, length us, event | category | flops | bytes accessed | tf_op | source)
XLA Modules:
  0.0 80.6 jit_solution(6847999021227292940)
XLA Ops:
  0.0 0.0 copy-start
  0.8 0.0 copy-start.2
  0.8 1.4 %copy-done.2 = bf16[512,1536]{1,0:T(8,128)(2,1)S(1)} copy-done((bf16[512,1536]{1,0:T(8,128)(2,1)S(1)}, bf16[512,1536]{1,0:T(8,128)(2,1)}, u32[]{:S(2)}) %copy-start.2) | copy-done | bytes 1572888
  2.2 0.0 copy-start.3
  2.2 1.2 %copy-done.3 = bf16[1,1024,512]{2,1,0:T(8,128)(2,1)S(1)} copy-done((bf16[1,1024,512]{2,1,0:T(8,128)(2,1)S(1)}, bf16[1,1024,512]{2,1,0:T(8,128)(2,1)}, u32[]{:S(2)}) %copy-start.3) | copy-done | bytes 1048600
  3.4 0.0 copy-start.4
  3.4 1.0 %copy-done.4 = bf16[512,512]{1,0:T(8,128)(2,1)S(1)} copy-done((bf16[512,512]{1,0:T(8,128)(2,1)S(1)}, bf16[512,512]{1,0:T(8,128)(2,1)}, u32[]{:S(2)}) %copy-start.4) | copy-done | bytes 524312
  4.5 0.0 copy-start.5
  4.5 1.0 %copy-done.5 = bf16[512,512]{1,0:T(8,128)(2,1)S(1)} copy-done((bf16[512,512]{1,0:T(8,128)(2,1)S(1)}, bf16[512,512]{1,0:T(8,128)(2,1)}, u32[]{:S(2)}) %copy-start.5) | copy-done | bytes 524312
  5.5 0.0 copy-start.6
  5.5 0.8 copy-done.6
  6.3 0.0 copy-start.7
  6.3 0.7 copy-done.7
  7.0 0.0 copy-start.8
  7.0 0.7 copy-done.8
  7.6 0.0 copy-start.9
  7.6 0.7 copy-done.9
  8.3 0.0 copy-start.10
  8.3 0.7 copy-done.10
  9.0 63.9 %front.1 = (bf16[1024,512]{1,0:T(8,128)(2,1)S(1)}, f32[8,512]{1,0:T(8,128)S(1)}) custom-call(bf16[1,1024,512]{2,1,0:T(8,128)(2,1)S(1)} %copy-done.3, s32[1,1024]{1,0:T(1,128)S(1)} %copy-done.7, s32[1,1]{1,0:T(1,128)S(6)} %copy.13.counts_hbm, bf16[27,512]{1,0:T(8,128)(2,1)S(1)} %copy-done.6, bf16[512,512]{1,0:T(8,128)(2,1)S(1)} %copy-done.4, ...), custom_call_target="tpu_custom_call" | custom-call | tf_op jit(solution)/shard_map/front/pallas_call | solution.py:404
  72.9 0.0 copy-done
  72.9 0.0 copy-start.1
  72.9 1.6 %copy-done.1 = bf16[2048,512]{1,0:T(8,128)(2,1)S(1)} copy-done((bf16[2048,512]{1,0:T(8,128)(2,1)S(1)}, bf16[2048,512]{1,0:T(8,128)(2,1)}, u32[]{:S(2)}) %copy-start.1) | copy-done | bytes 2097176
  74.5 6.1 %back.1 = bf16[1,1024,512]{2,1,0:T(8,128)(2,1)} custom-call(bf16[1024,512]{1,0:T(8,128)(2,1)S(1)} %get-tuple-element.7.second, f32[8,512]{1,0:T(8,128)S(1)} %get-tuple-element.8.aside, bf16[512,2048]{1,0:T(8,128)(2,1)S(1)} %copy-done, bf16[2048,512]{1,0:T(8,128)(2,1)S(1)} %copy-done.1), custom_call_target="tpu_custom_call" | custom-call | tf_op jit(solution)/shard_map/back/pallas_call | solution.py:464
Async XLA Ops:
  0.0 72.9 %copy-start = (bf16[512,2048]{1,0:T(8,128)(2,1)S(1)}, bf16[512,2048]{1,0:T(8,128)(2,1)}, u32[]{:S(2)}) copy-start(bf16[512,2048]{1,0:T(8,128)(2,1)} %mlp_in.1) | copy-start | bytes 6291460
  0.8 1.4 %copy-start.2 = (bf16[512,1536]{1,0:T(8,128)(2,1)S(1)}, bf16[512,1536]{1,0:T(8,128)(2,1)}, u32[]{:S(2)}) copy-start(bf16[512,1536]{1,0:T(8,128)(2,1)} %qkv_hbm.1) | copy-start | bytes 4718596
  2.2 1.2 %copy-start.3 = (bf16[1,1024,512]{2,1,0:T(8,128)(2,1)S(1)}, bf16[1,1024,512]{2,1,0:T(8,128)(2,1)}, u32[]{:S(2)}) copy-start(bf16[1,1024,512]{2,1,0:T(8,128)(2,1)} %points_hbm.1) | copy-start | bytes 3145732
  3.4 1.0 %copy-start.4 = (bf16[512,512]{1,0:T(8,128)(2,1)S(1)}, bf16[512,512]{1,0:T(8,128)(2,1)}, u32[]{:S(2)}) copy-start(bf16[512,512]{1,0:T(8,128)(2,1)} %cpe_w_hbm.1) | copy-start | bytes 1572868
  4.5 1.0 %copy-start.5 = (bf16[512,512]{1,0:T(8,128)(2,1)S(1)}, bf16[512,512]{1,0:T(8,128)(2,1)}, u32[]{:S(2)}) copy-start(bf16[512,512]{1,0:T(8,128)(2,1)} %proj_hbm.1) | copy-start | bytes 1572868
  5.5 0.8 copy-start.6
  6.3 0.7 copy-start.7
  7.0 0.7 copy-start.8
  7.6 0.7 copy-start.9
  8.3 0.7 copy-start.10
  72.9 1.6 %copy-start.1 = (bf16[2048,512]{1,0:T(8,128)(2,1)S(1)}, bf16[2048,512]{1,0:T(8,128)(2,1)}, u32[]{:S(2)}) copy-start(bf16[2048,512]{1,0:T(8,128)(2,1)} %mlp_out.1) | copy-start | bytes 6291460

commit v2 on v1

--- a/solution.py
+++ b/solution.py
@@ -18,8 +18,12 @@
 VOX = 2048
 PLANE = VY * VZ
 NEG = -1e30
+INNER = (VX - 2) * PLANE
+EDGE = 2 * PLANE + (VX - 2) * 2 * VZ
 CQ = 256
 UNROLL = 4
+FRONT_VMEM = 63 * 2**20
+BACK_VMEM = 63 * 2**20
 
 
 def dot(a, b):
@@ -65,8 +69,13 @@
     proj_w,
     wt,
     grid,
+    face_out,
+    face_in,
     taps,
     conv,
+    edge_sum,
+    edge,
+    pos,
     first,
     normed,
     far,
@@ -141,7 +150,6 @@
         )
 
     inner_y = pl.ds(1, VY)
-    inner_x = pl.ds(1, VX)
     halo_x = [
         remote(0, grid.at[1, inner_y], grid.at[VX + 1, inner_y], (low_x, by)),
         remote(1, grid.at[VX, inner_y], grid.at[0, inner_y], (high_x, by)),
@@ -152,8 +160,8 @@
         remote(6, count_out, count_in, (high_x, by)),
     ]
     halo_y = [
-        remote(7, grid.at[inner_x, 1], grid.at[inner_x, VY + 1], (bx, low_y)),
-        remote(8, grid.at[inner_x, VY], grid.at[inner_x, 0], (bx, high_y)),
+        remote(7, face_out.at[0], face_in.at[1], (bx, low_y)),
+        remote(8, face_out.at[1], face_in.at[0], (bx, high_y)),
     ]
     low_half, high_half = pl.ds(0, HALF), pl.ds(HALF, HALF)
     to_low = remote(9, normed.at[low_half], far.at[high_half], (low_x, by))
@@ -168,56 +176,125 @@
 
     loads[2].wait()
 
-    def scatter(plane):
-        row = lax.broadcasted_iota(jnp.int32, (PLANE, ROWS), 0) + plane * PLANE
+    def scatter(first, second):
+        row = lax.broadcasted_iota(jnp.int32, (2 * PLANE, ROWS), 0)
+        row = row + jnp.where(row < PLANE, first * PLANE, (second - 1) * PLANE)
         hot = jnp.where(row == where_to, 1.0, 0.0).astype(BF)
-        grid[plane + 1, 1 : VY + 1] = dot(hot, feats[...]).astype(BF).reshape(VY, VZ, C)
-
-    scatter(0)
-    scatter(VX - 1)
+        block = dot(hot, feats[...]).astype(BF).reshape(2, VY, VZ, C)
+        for i, plane in enumerate((first, second)):
+            grid[plane + 1, 1 : VY + 1] = block[i]
+            face_out[0, plane] = block[i, 0]
+            face_out[1, plane] = block[i, VY - 1]
+
+    scatter(0, VX - 1)
     pl.semaphore_wait(barrier, 8)
     for copy in halo_x:
         copy.start()
 
-    def scatter_step(plane, carry):
-        scatter(plane)
+    def scatter_step(i, carry):
+        scatter(2 * i + 1, 2 * i + 2)
         return carry
 
-    lax.fori_loop(1, VX - 1, scatter_step, 0)
+    lax.fori_loop(0, VX // 2 - 1, scatter_step, 0)
     for copy in halo_y:
         copy.start()
 
     loads[3].wait()
     taps[...] = depth[...].astype(F32)
 
-    def conv_rows(x, lanes, y_first, y_count):
-        weight = [taps[pl.ds(i, 1), lanes] for i in range(27)]
-        z = lax.broadcasted_iota(jnp.int32, (VZ, 128), 0)
+    z = lax.broadcasted_iota(jnp.int32, (VZ, 128), 0)
+
+    def conv_rows(x, end, lanes, y_first, y_count, own):
         parts = [[None] * 3 for _ in range(y_count)]
         for off_x in range(3):
+            x_out = off_x - 1 == end and end != 0
             for row in range(y_count + 2):
-                block = grid[x + off_x, y_first + row, :, lanes].astype(F32)
+                y = y_first + row - 1
+                y_out = y < 0 or y >= VY
+                if own == (x_out or y_out):
+                    continue
+                if y_out and not x_out:
+                    block = face_in[0 if y < 0 else 1, x + off_x - 1, :, lanes].astype(F32)
+                else:
+                    block = grid[x + off_x, y + 1, :, lanes].astype(F32)
                 for i in range(y_count):
                     off_y = row - i
                     if 0 <= off_y <= 2:
                         for off_z in range(3):
-                            term = block * weight[9 * off_x + 3 * off_y + off_z]
+                            term = block * taps[pl.ds(9 * off_x + 3 * off_y + off_z, 1), lanes]
                             held = parts[i][off_z]
                             parts[i][off_z] = term if held is None else held + term
-        for i in range(y_count):
-            before, same, after = parts[i]
+        sums = []
+        for before, same, after in parts:
             before = jnp.where(z == 0, 0.0, pltpu.roll(before, 1, 0))
             after = jnp.where(z == VZ - 1, 0.0, pltpu.roll(after, VZ - 1, 0))
-            start = pl.multiple_of(x * PLANE + (y_first + i) * VZ, VZ)
-            conv[pl.ds(start, VZ), lanes] = (before + same + after).astype(BF)
+            sums.append(before + same + after)
+        return sums
+
+    def edge_rows(x, end, y):
+        if end:
+            return pl.ds((0 if end < 0 else PLANE) + y * VZ, VZ)
+        start = 2 * PLANE + (x - 1) * 2 * VZ + (0 if y == 0 else VZ)
+        return pl.ds(pl.multiple_of(start, VZ), VZ)
+
+    def lane_tile(i):
+        return pl.ds(pl.multiple_of(i * 128, 128), 128)
 
     def inner_step(i, carry):
-        lanes = pl.ds(pl.multiple_of(lax.rem(i, 4) * 128, 128), 128)
-        for y in range(1, VY - 1, 2):
-            conv_rows(lax.div(i, 4) + 1, lanes, y, 2)
+        lanes = lane_tile(lax.rem(i, 4))
+        x = lax.div(i, 4) + 1
+        for first_y in range(0, VY, 2):
+            for y, total in enumerate(conv_rows(x, 0, lanes, first_y, 2, True), first_y):
+                if y in (0, VY - 1):
+                    edge_sum[edge_rows(x, 0, y), lanes] = total
+                else:
+                    start = pl.multiple_of((x - 1) * PLANE + y * VZ, VZ)
+                    conv[pl.ds(start, VZ), lanes] = total.astype(BF)
         return carry
 
     lax.fori_loop(0, 4 * (VX - 2), inner_step, 0)
+
+    def end_step(i, carry):
+        lanes = lane_tile(i)
+        for x, end in ((0, -1), (VX - 1, 1)):
+            for first_y in range(0, VY, 2):
+                for y, total in enumerate(conv_rows(x, end, lanes, first_y, 2, True), first_y):
+                    edge_sum[edge_rows(x, end, y), lanes] = total
+        return carry
+
+    lax.fori_loop(0, 4, end_step, 0)
+
+    for x in range(VX - 2):
+        for y in (0, VY - 1):
+            conv[x * PLANE + y * VZ : x * PLANE + (y + 1) * VZ] = jnp.zeros((VZ, C), BF)
+
+    def one_hot(index, half, first, size):
+        column = jnp.concatenate(
+            [
+                jnp.broadcast_to(index[:, half * HALF + i * 128 : half * HALF + (i + 1) * 128], (128, 128)).T
+                for i in range(HALF // 128)
+            ],
+            axis=0,
+        )
+        pieces = [
+            jnp.where(
+                column == (lax.broadcasted_iota(jnp.int32, (1, 128), 1) + (first + i * 128)).astype(F32),
+                1.0,
+                0.0,
+            ).astype(BF)
+            for i in range(size // 128)
+        ]
+        return jnp.concatenate(pieces, axis=1)
+
+    voxel = voxels[...]
+    inner_index = (voxel - PLANE).astype(F32)
+    for half in range(2):
+        total = None
+        for part in range(INNER // HALF):
+            hot = one_hot(inner_index, half, part * HALF, HALF)
+            term = dot(hot, conv[part * HALF : (part + 1) * HALF])
+            total = term if total is None else total + term
+        pos[half * HALF : (half + 1) * HALF] = total.astype(BF)
 
     for load in loads[4:]:
         load.wait()
@@ -227,7 +304,8 @@
     for copy in halo_x + halo_y:
         copy.wait()
     zero_x = jnp.zeros((VY + 2, VZ, C), BF)
-    zero_y = jnp.zeros((VX + 2, VZ, C), BF)
+    zero_y = jnp.zeros((VX, VZ, C), BF)
+    zero_row = jnp.zeros((VZ, C), BF)
 
     @pl.when(bx == 0)
     def _():
@@ -239,46 +317,50 @@
 
     @pl.when(by == 0)
     def _():
-        grid[:, 0] = zero_y
+        face_in[0] = zero_y
+        grid[0, 0] = zero_row
+        grid[VX + 1, 0] = zero_row
 
     @pl.when(by == n_by - 1)
     def _():
-        grid[:, VY + 1] = zero_y
+        face_in[1] = zero_y
+        grid[0, VY + 1] = zero_row
+        grid[VX + 1, VY + 1] = zero_row
 
     def outer_step(i, carry):
-        lanes = pl.ds(pl.multiple_of(lax.rem(i, 4) * 128, 128), 128)
-        for y in range(0, VY, 2):
-            conv_rows(lax.div(i, 4) * (VX - 1), lanes, y, 2)
+        lanes = lane_tile(i)
+        for x, end in ((0, -1), (VX - 1, 1)):
+            for first_y in range(0, VY, 2):
+                for y, total in enumerate(conv_rows(x, end, lanes, first_y, 2, False), first_y):
+                    rows = edge_rows(x, end, y)
+                    edge[rows, lanes] = (edge_sum[rows, lanes] + total).astype(BF)
         return carry
 
-    lax.fori_loop(0, 8, outer_step, 0)
+    lax.fori_loop(0, 4, outer_step, 0)
 
     def side_step(i, carry):
-        lanes = pl.ds(pl.multiple_of(lax.rem(i, 4) * 128, 128), 128)
+        lanes = lane_tile(lax.rem(i, 4))
+        x = lax.div(i, 4) + 1
         for y in (0, VY - 1):
-            conv_rows(lax.div(i, 4) + 1, lanes, y, 1)
+            rows = edge_rows(x, 0, y)
+            total = conv_rows(x, 0, lanes, y, 1, False)[0]
+            edge[rows, lanes] = (edge_sum[rows, lanes] + total).astype(BF)
         return carry
 
     lax.fori_loop(0, 4 * (VX - 2), side_step, 0)
 
+    at_x, at_y = lax.div(voxel, PLANE), lax.rem(lax.div(voxel, VZ), VY)
+    at_z = lax.rem(voxel, VZ)
+    side = 2 * PLANE + (at_x - 1) * 2 * VZ + at_z
+    edge_index = jnp.where(at_y == 0, side, jnp.where(at_y == VY - 1, side + VZ, -1))
+    edge_index = jnp.where(at_x == VX - 1, voxel - (VX - 2) * PLANE, edge_index)
+    edge_index = jnp.where(at_x == 0, voxel, edge_index).astype(F32)
+
     def gather(half):
-        total = None
-        for part in range(4):
-            lane = lax.broadcasted_iota(jnp.int32, (HALF, HALF), 1) + part * HALF
-            column = jnp.concatenate(
-                [
-                    jnp.broadcast_to(
-                        voxels[:, half * HALF + i * 128 : half * HALF + (i + 1) * 128].astype(F32),
-                        (128, 128),
-                    ).T
-                    for i in range(4)
-                ],
-                axis=0,
-            ).astype(jnp.int32)
-            hot = jnp.where(jnp.concatenate([column] * 4, axis=1) == lane, 1.0, 0.0).astype(BF)
-            term = dot(hot, conv[part * HALF : (part + 1) * HALF])
-            total = term if total is None else total + term
         rows = slice(half * HALF, (half + 1) * HALF)
+        total = pos[rows].astype(F32)
+        total = total + dot(one_hot(edge_index, half, 0, 512), edge[0:512])
+        total = total + dot(one_hot(edge_index, half, 512, 256)[:, : EDGE - 512], edge[512:EDGE])
         branch = layer_norm(dot(total.astype(BF), cpe_w[...])) * cpe_gain[...].reshape(1, C).astype(F32)
         here = (feats[rows].astype(F32) + branch).astype(BF)
         first[rows] = here
@@ -374,15 +456,36 @@
     return half + half * lax.erf(x * 0.7071067811865476)
 
 
-def back_kernel(second, aside, mlp_in, mlp_out, out):
+def back_kernel(second_hbm, aside_hbm, mlp_in_hbm, mlp_out_hbm, out_hbm, second, aside, mlp_in, mlp_out, out, sem):
+    loads = [
+        pltpu.make_async_copy(source, held, sem.at[i])
+        for i, (source, held) in enumerate(
+            (
+                (second_hbm, second),
+                (aside_hbm, aside),
+                (mlp_in_hbm, mlp_in),
+                (mlp_out_hbm, mlp_out),
+            )
+        )
+    ]
+    for load in loads:
+        load.start()
+    loads[0].wait()
+    loads[1].wait()
     total = second[...].astype(F32)
     normed = (layer_norm(total) * aside[0:1, :]).astype(BF)
+    loads[2].wait()
     for part in range(4):
         cols = slice(part * 512, (part + 1) * 512)
         hidden = gelu(dot(normed, mlp_in[:, cols])).astype(BF)
+        if part == 0:
+            loads[3].wait()
         total = total + dot(hidden, mlp_out[cols, :])
     row_id = lax.broadcasted_iota(jnp.int32, (ROWS, C), 0).astype(F32)
-    out[0] = jnp.where(row_id < aside[1:2, :], total, 0.0).astype(BF)
+    out[...] = jnp.where(row_id < aside[1:2, :], total, 0.0).astype(BF)
+    store = pltpu.make_async_copy(out, out_hbm.at[0], sem.at[4])
+    store.start()
+    store.wait()
 
 
 def per_device(
@@ -422,8 +525,13 @@
             pltpu.VMEM((C, C), BF),
             pltpu.VMEM((2 * C, C), BF),
             pltpu.VMEM((VX + 2, VY + 2, VZ, C), BF),
+            pltpu.VMEM((2, VX, VZ, C), BF),
+            pltpu.VMEM((2, VX, VZ, C), BF),
             pltpu.VMEM((27, C), F32),
-            pltpu.VMEM((VOX, C), BF),
+            pltpu.VMEM((INNER, C), BF),
+            pltpu.VMEM((EDGE, C), F32),
+            pltpu.VMEM((EDGE, C), BF),
+            pltpu.VMEM((ROWS, C), BF),
             pltpu.VMEM((ROWS, C), BF),
             pltpu.VMEM((ROWS, C), BF),
             pltpu.VMEM((ROWS, C), BF),
@@ -446,7 +554,7 @@
             pltpu.SemaphoreType.DMA((11,)),
         ],
         compiler_params=pltpu.CompilerParams(
-            collective_id=0, has_side_effects=True, vmem_limit_bytes=48 * 2**20
+            collective_id=0, has_side_effects=True, vmem_limit_bytes=FRONT_VMEM
         ),
         name="front",
     )(
@@ -464,9 +572,17 @@
     return pl.pallas_call(
         back_kernel,
         out_shape=jax.ShapeDtypeStruct((1, ROWS, C), BF),
-        in_specs=[vmem] * 4,
-        out_specs=vmem,
-        compiler_params=pltpu.CompilerParams(vmem_limit_bytes=48 * 2**20),
+        in_specs=[hbm] * 4,
+        out_specs=hbm,
+        scratch_shapes=[
+            pltpu.VMEM((ROWS, C), BF),
+            pltpu.VMEM((8, C), F32),
+            pltpu.VMEM((C, 4 * C), BF),
+            pltpu.VMEM((4 * C, C), BF),
+            pltpu.VMEM((ROWS, C), BF),
+            pltpu.SemaphoreType.DMA((5,)),
+        ],
+        compiler_params=pltpu.CompilerParams(vmem_limit_bytes=BACK_VMEM),
         name="back",
     )(second, aside, mlp_in, mlp_out)
 

time: 81.9 us -> 72.9 us (0.89); the launches traced: 80.6 us -> 72.8 us
  local copies, waits for them, and re-layouts: 9.78 us -> 0 us
  Pallas kernels: 70 us -> 72 us
    unnamed x22 -> x0, local copies, waits for them, and re-layouts: 9.78 us -> none
    pallas_call x1, Pallas kernels: 6.07 us -> 7.84 us  [per_device(): pl.pallas_call(back_kernel, out_shape=jax.ShapeDtypeStruct((1, ROWS, C),...]
where the time goes in v2:
time: 72.9 us; the launch traced here: 72.8 us
  Pallas kernels  72 us (99%)
  between operations  0.84 us (1%)
    pallas_call x1, Pallas kernels, per_device(): pl.pallas_call(front_kernel, out_shape=(jax.ShapeDtypeStruct((ROWS, C), B...  64.2 us
    pallas_call x1, Pallas kernels, per_device(): pl.pallas_call(back_kernel, out_shape=jax.ShapeDtypeStruct((1, ROWS, C),...  7.84 us

profile of v2, /device:TPU:1, one launch (start us, length us, event | category | flops | bytes accessed | tf_op | source)
XLA Modules:
  0.0 72.8 jit_solution(13823259058529537485)
XLA Ops:
  0.7 64.2 %front.1 = (bf16[1024,512]{1,0:T(8,128)(2,1)}, f32[8,512]{1,0:T(8,128)}) custom-call(bf16[1,1024,512]{2,1,0:T(8,128)(2,1)} %points_hbm.1, s32[1,1024]{1,0:T(1,128)} %voxels_hbm.1, s32[1,1]{1,0:T(1,128)S(6)} %copy.13.counts_hbm, bf16[27,512]{1,0:T(8,128)(2,1)} %depth_hbm.1, bf16[512,512]{1,0:T(8,128)(2,1)} %cpe_w_hbm.1, bf16[512]{0:T(512)(128)(2,1)} %cpe_gain_hbm.1, ...), custom_call_target="tpu_custom_call" | custom-call | tf_op jit(solution)/shard_map/front/pallas_call | solution.py:507
  64.8 7.8 %back.1 = bf16[1,1024,512]{2,1,0:T(8,128)(2,1)} custom-call(bf16[1024,512]{1,0:T(8,128)(2,1)} %get-tuple-element.7.second_hbm, f32[8,512]{1,0:T(8,128)} %get-tuple-element.8.aside_hbm, bf16[512,2048]{1,0:T(8,128)(2,1)} %mlp_in_hbm.1, bf16[2048,512]{1,0:T(8,128)(2,1)} %mlp_out_hbm.1), custom_call_target="tpu_custom_call" | custom-call | tf_op jit(solution)/shard_map/back/pallas_call | solution.py:572

commit v3 on v2

--- a/solution.py
+++ b/solution.py
@@ -84,8 +84,7 @@
     vt,
     far_keys,
     far_vt,
-    bias,
-    ones_row,
+    ones,
     scores,
     tops,
     part_o,
@@ -378,18 +377,22 @@
     aside[0:1, :] = gain2[...].reshape(1, C).astype(F32)
     aside[1:2, :] = jnp.broadcast_to(count, (1, C))
 
-    row_id = (lax.broadcasted_iota(jnp.int32, (HALF, 128), 0) + HALF).astype(F32)
-    lane_id = lax.broadcasted_iota(jnp.int32, (HALF, 128), 1)
-    bias[0] = jnp.where((lane_id == 0) & (row_id >= count), NEG, 0.0).astype(BF)
-    bias[1] = jnp.where((lane_id == 0) & (row_id >= count_in[0:1, :]), NEG, 0.0).astype(BF)
-    ones_row[...] = jnp.where(
-        lax.broadcasted_iota(jnp.int32, (128, CQ), 0) == 0, 1.0, 0.0
-    ).astype(BF)
+    row_id = (lax.broadcasted_iota(jnp.int32, (HALF, 1), 0) + HALF).astype(F32)
+    col_id = (lax.broadcasted_iota(jnp.int32, (1, HALF), 1) + HALF).astype(F32)
+
+    def drop_invalid(k_ref, v_ref, start, total, which):
+        here = slice(start, start + HALF)
+        held = k_ref[here].astype(F32)
+        k_ref[here] = jnp.where(row_id < total, held, held[0:1]).astype(BF)
+        v_ref[:, here] = jnp.where(col_id < total, v_ref[:, here].astype(F32), 0.0).astype(BF)
+        ones[which] = jnp.broadcast_to(jnp.where(col_id < total, 1.0, 0.0), (16, HALF)).astype(BF)
+
+    drop_invalid(keys, vt, HALF, count, 0)
 
     lane_head = lax.broadcasted_iota(jnp.int32, (1, 128), 1) // 16
-    ones16 = jnp.ones((16, HALF), BF)
-
-    def attention(k_ref, v_ref, biased, which, finish):
+    all_ones = jnp.ones((16, HALF), BF)
+
+    def attention(k_ref, v_ref, partial, which, finish):
         def step(h, before, now):
             other = 1 - now
             lanes = pl.ds(pl.multiple_of(lax.div(h, 8) * 128, 128), 128)
@@ -400,15 +403,12 @@
                 rows = slice(b * HALF, (b + 1) * HALF)
                 k_h = k_ref[rows, lanes]
                 k_h = jnp.where(mine, k_h, jnp.zeros_like(k_h))
-                if b == biased:
-                    k_h = jnp.concatenate([k_h, bias[which]], axis=1)
                 if before is not None:
-                    w = jnp.concatenate([v_ref[head_rows, rows], ones16], axis=0)
+                    counted = ones[which] if b == partial else all_ones
+                    w = jnp.concatenate([v_ref[head_rows, rows], counted], axis=0)
                 for part in range(HALF // CQ):
                     cols = slice(b * HALF + part * CQ, b * HALF + (part + 1) * CQ)
                     q_g = qt[lanes, cols]
-                    if b == biased:
-                        q_g = jnp.concatenate([q_g, ones_row[...]], axis=0)
                     s = dot(k_h, q_g)
                     scores[now, :, cols] = s
                     tops[now, 0:1, cols] = jnp.max(s, axis=0, keepdims=True)
@@ -438,6 +438,7 @@
     to_high.wait()
     far_keys[...] = dot(far[...], qkv_w[:, C : 2 * C]).astype(BF)
     far_vt[...] = dot_nt(wt[C : 2 * C], far[...]).astype(BF)
+    drop_invalid(far_keys, far_vt, 0, count_in[0:1, 0:1], 1)
 
     def merge(h, head_rows, cols, top, acc):
         near_top = part_ml[h, 0:1, cols]
@@ -540,8 +541,7 @@
             pltpu.VMEM((C, ROWS), BF),
             pltpu.VMEM((ROWS, C), BF),
             pltpu.VMEM((C, ROWS), BF),
-            pltpu.VMEM((2, HALF, 128), BF),
-            pltpu.VMEM((128, CQ), BF),
+            pltpu.VMEM((2, 16, HALF), BF),
             pltpu.VMEM((2, HALF, ROWS), F32),
             pltpu.VMEM((2, 8, ROWS), F32),
             pltpu.VMEM((C, ROWS), F32),

time: 72.9 us -> 70.9 us (0.973)
  Pallas kernels: 72 us -> 70 us
    pallas_call x1, Pallas kernels: 64.2 us -> 62.2 us  [per_device(): pl.pallas_call(front_kernel, out_shape=(jax.ShapeDtypeStruct((ROWS, C), B...]
where the time goes in v3:
time: 70.9 us; the launch traced here: 70.8 us
  Pallas kernels  70 us (99%)
  between operations  0.84 us (1%)
    pallas_call x1, Pallas kernels, per_device(): pl.pallas_call(front_kernel, out_shape=(jax.ShapeDtypeStruct((ROWS, C), B...  62.2 us
    pallas_call x1, Pallas kernels, per_device(): pl.pallas_call(back_kernel, out_shape=jax.ShapeDtypeStruct((1, ROWS, C),...  7.84 us

profile of v3, /device:TPU:1, one launch (start us, length us, event | category | flops | bytes accessed | tf_op | source)
XLA Modules:
  0.0 70.8 jit_solution(12121542702169319245)
XLA Ops:
  0.7 62.2 %front.1 = (bf16[1024,512]{1,0:T(8,128)(2,1)}, f32[8,512]{1,0:T(8,128)}) custom-call(bf16[1,1024,512]{2,1,0:T(8,128)(2,1)} %points_hbm.1, s32[1,1024]{1,0:T(1,128)} %voxels_hbm.1, s32[1,1]{1,0:T(1,128)S(6)} %copy.13.counts_hbm, bf16[27,512]{1,0:T(8,128)(2,1)} %depth_hbm.1, bf16[512,512]{1,0:T(8,128)(2,1)} %cpe_w_hbm.1, bf16[512]{0:T(512)(128)(2,1)} %cpe_gain_hbm.1, ...), custom_call_target="tpu_custom_call" | custom-call | tf_op jit(solution)/shard_map/front/pallas_call | solution.py:508
  62.8 7.8 %back.1 = bf16[1,1024,512]{2,1,0:T(8,128)(2,1)} custom-call(bf16[1024,512]{1,0:T(8,128)(2,1)} %get-tuple-element.7.second_hbm, f32[8,512]{1,0:T(8,128)} %get-tuple-element.8.aside_hbm, bf16[512,2048]{1,0:T(8,128)(2,1)} %mlp_in_hbm.1, bf16[2048,512]{1,0:T(8,128)(2,1)} %mlp_out_hbm.1), custom_call_target="tpu_custom_call" | custom-call | tf_op jit(solution)/shard_map/back/pallas_call | solution.py:572

commit v4 on v3

--- a/solution.py
+++ b/solution.py
@@ -135,7 +135,7 @@
             )
         )
     ]
-    for load in loads:
+    for load in loads[:7]:
         load.start()
 
     def remote(i, source, target, where):
@@ -174,6 +174,8 @@
     where_to = jnp.where(slot.astype(F32) < count, voxels[...], VOX)
 
     loads[2].wait()
+    for load in loads[7:]:
+        load.start()
 
     def scatter(first, second):
         row = lax.broadcasted_iota(jnp.int32, (2 * PLANE, ROWS), 0)
@@ -182,21 +184,31 @@
         block = dot(hot, feats[...]).astype(BF).reshape(2, VY, VZ, C)
         for i, plane in enumerate((first, second)):
             grid[plane + 1, 1 : VY + 1] = block[i]
-            face_out[0, plane] = block[i, 0]
-            face_out[1, plane] = block[i, VY - 1]
-
-    scatter(0, VX - 1)
+        return block
+
+    ends = scatter(0, VX - 1)
     pl.semaphore_wait(barrier, 8)
     for copy in halo_x:
         copy.start()
 
+    face = lax.broadcasted_iota(jnp.int32, ((VX - 2) * 2 * VZ, ROWS), 0)
+    in_plane = lax.rem(face, 2 * VZ)
+    face = PLANE + lax.div(face, 2 * VZ) * PLANE + in_plane
+    face = face + jnp.where(in_plane < VZ, 0, PLANE - 2 * VZ)
+    hot = jnp.where(face == where_to, 1.0, 0.0).astype(BF)
+    sides = dot(hot, feats[...]).astype(BF).reshape(VX - 2, 2, VZ, C)
+    for i in range(2):
+        face_out[i, 1 : VX - 1] = sides[:, i]
+        face_out[i, 0] = ends[0, i * (VY - 1)]
+        face_out[i, VX - 1] = ends[1, i * (VY - 1)]
+    for copy in halo_y:
+        copy.start()
+
     def scatter_step(i, carry):
         scatter(2 * i + 1, 2 * i + 2)
         return carry
 
     lax.fori_loop(0, VX // 2 - 1, scatter_step, 0)
-    for copy in halo_y:
-        copy.start()
 
     loads[3].wait()
     taps[...] = depth[...].astype(F32)

time: 70.9 us -> 71.3 us (level)
  no operation moved by 1% of the time
where the time goes in v4:
time: 71.3 us; the launch traced here: 71.2 us
  Pallas kernels  70.4 us (99%)
  between operations  0.84 us (1%)
    pallas_call x1, Pallas kernels, per_device(): pl.pallas_call(front_kernel, out_shape=(jax.ShapeDtypeStruct((ROWS, C), B...  62.5 us
    pallas_call x1, Pallas kernels, per_device(): pl.pallas_call(back_kernel, out_shape=jax.ShapeDtypeStruct((1, ROWS, C),...  7.84 us

profile of v4, /device:TPU:1, one launch (start us, length us, event | category | flops | bytes accessed | tf_op | source)
XLA Modules:
  0.0 71.2 jit_solution(7986811831749953507)
XLA Ops:
  0.7 62.5 %front.1 = (bf16[1024,512]{1,0:T(8,128)(2,1)}, f32[8,512]{1,0:T(8,128)}) custom-call(bf16[1,1024,512]{2,1,0:T(8,128)(2,1)} %points_hbm.1, s32[1,1024]{1,0:T(1,128)} %voxels_hbm.1, s32[1,1]{1,0:T(1,128)S(6)} %copy.13.counts_hbm, bf16[27,512]{1,0:T(8,128)(2,1)} %depth_hbm.1, bf16[512,512]{1,0:T(8,128)(2,1)} %cpe_w_hbm.1, bf16[512]{0:T(512)(128)(2,1)} %cpe_gain_hbm.1, ...), custom_call_target="tpu_custom_call" | custom-call | tf_op jit(solution)/shard_map/front/pallas_call | solution.py:520
  63.2 7.8 %back.1 = bf16[1,1024,512]{2,1,0:T(8,128)(2,1)} custom-call(bf16[1024,512]{1,0:T(8,128)(2,1)} %get-tuple-element.7.second_hbm, f32[8,512]{1,0:T(8,128)} %get-tuple-element.8.aside_hbm, bf16[512,2048]{1,0:T(8,128)(2,1)} %mlp_in_hbm.1, bf16[2048,512]{1,0:T(8,128)(2,1)} %mlp_out_hbm.1), custom_call_target="tpu_custom_call" | custom-call | tf_op jit(solution)/shard_map/back/pallas_call | solution.py:584

commit v5 on v3

--- a/solution.py
+++ b/solution.py
@@ -21,7 +21,7 @@
 INNER = (VX - 2) * PLANE
 EDGE = 2 * PLANE + (VX - 2) * 2 * VZ
 CQ = 256
-UNROLL = 4
+UNROLL = 8
 FRONT_VMEM = 63 * 2**20
 BACK_VMEM = 63 * 2**20
 

time: 70.9 us -> 69.7 us (0.983)
  Pallas kernels: 70 us -> 68.7 us
    pallas_call x1, Pallas kernels: 62.2 us -> 60.9 us  [per_device(): pl.pallas_call(front_kernel, out_shape=(jax.ShapeDtypeStruct((ROWS, C), B...]
where the time goes in v5:
time: 69.7 us; the launch traced here: 69.6 us
  Pallas kernels  68.7 us (99%)
  between operations  0.84 us (1%)
    pallas_call x1, Pallas kernels, per_device(): pl.pallas_call(front_kernel, out_shape=(jax.ShapeDtypeStruct((ROWS, C), B...  60.9 us
    pallas_call x1, Pallas kernels, per_device(): pl.pallas_call(back_kernel, out_shape=jax.ShapeDtypeStruct((1, ROWS, C),...  7.84 us

profile of v5, /device:TPU:1, one launch (start us, length us, event | category | flops | bytes accessed | tf_op | source)
XLA Modules:
  0.0 69.6 jit_solution(5795033126327612232)
XLA Ops:
  0.7 60.9 %front.1 = (bf16[1024,512]{1,0:T(8,128)(2,1)}, f32[8,512]{1,0:T(8,128)}) custom-call(bf16[1,1024,512]{2,1,0:T(8,128)(2,1)} %points_hbm.1, s32[1,1024]{1,0:T(1,128)} %voxels_hbm.1, s32[1,1]{1,0:T(1,128)S(6)} %copy.13.counts_hbm, bf16[27,512]{1,0:T(8,128)(2,1)} %depth_hbm.1, bf16[512,512]{1,0:T(8,128)(2,1)} %cpe_w_hbm.1, bf16[512]{0:T(512)(128)(2,1)} %cpe_gain_hbm.1, ...), custom_call_target="tpu_custom_call" | custom-call | tf_op jit(solution)/shard_map/front/pallas_call | solution.py:508
  61.5 7.8 %back.1 = bf16[1,1024,512]{2,1,0:T(8,128)(2,1)} custom-call(bf16[1024,512]{1,0:T(8,128)(2,1)} %get-tuple-element.7.second_hbm, f32[8,512]{1,0:T(8,128)} %get-tuple-element.8.aside_hbm, bf16[512,2048]{1,0:T(8,128)(2,1)} %mlp_in_hbm.1, bf16[2048,512]{1,0:T(8,128)(2,1)} %mlp_out_hbm.1), custom_call_target="tpu_custom_call" | custom-call | tf_op jit(solution)/shard_map/back/pallas_call | solution.py:572
